TPU v7x, 256 devices: a whole 4x4x8 slice. The times are simulated.
256 devices in a mesh: gx: 16 (over x, y), gz: 8 (over z), gy: 2 (over core).
Axes of the slice: x: 4, y: 4, z: 8, core: 2. Of those that a mesh axis runs over, the one named last changes fastest.
Arguments:
- blocks: bfloat16 [16, 8, 4, 96, 4096], P('gx', 'gz', 'gy'), may hold values from -6 to 6
- block_count: int32 [16, 8, 2], P('gx', 'gz', 'gy'), may hold values from 1 to 2, as said below
- neighbours: int32 [16, 8, 4, 26], P('gx', 'gz', 'gy'), may hold values from -1 to 15, as said below
- conv_weight: bfloat16 [48, 2592], replicated, may hold values from -0.125 to 0.125
- conv_bias: float32 [48], replicated, may hold values from -3 to 3
- head_weight: bfloat16 [48, 48], replicated, may hold values from -0.875 to 0.875
- head_bias: float32 [48], replicated, may hold values from -3 to 3
Outputs:
- features: bfloat16 [16, 8, 4, 48, 4096], P('gx', 'gz', 'gy')
Inputs may be any that keep to these rules, and one draw needn't show every extreme that they name: Each device's foreground blocks fill its first block_count slots; some device fills all 2. `neighbours`: -1 means no foreground block at that offset. Otherwise the value is u + 2 c: used slot u of the device reached from this one by the offset's steps along the axes whose bits are set in c (bit 0 x, bit 1 y, bit 2 z); bits are set only on axes where the offset is nonzero, and c = 0 names this device. Unused slots hold -1 everywhere. Each device's blocks sit at distinct positions of its own region of 2 x 2 x 4 block positions, and the links follow that geometry. The most is reached in every draw.
All inputs are finite; a program needn't handle non-finite values.
Results may differ from a plain program's by a relative error of at most 0.0046.
Values may be sent and summed in bfloat16 or wider, within the bound.
No kernel may reach another device: no remote copies, remote signals or barrier semaphores. Data moves between devices by JAX's collectives and lax.ppermute only.
A program may use at most 128 MiB of HBM per device.

v0:
```python
import jax
import jax.numpy as jnp
from jax import lax
from jax.experimental import pallas as pl
from jax.experimental.pallas import tpu as pltpu
from jax.sharding import PartitionSpec as P

CIN = 96
COUT = 48
EDGE = 16
PLANE = 256
VOX = 4096
SLOTS = 2
TAPS = 9
BF = jnp.bfloat16
F32 = jnp.float32

OWN_X, FAR_X, FAR_Y, OWN_Y, EDGE_Y, NEAR_SOURCES = 0, 4, 8, 10, 14, 18
FAR_Z, EDGE_Z, TURN_Z, Z_SOURCES = 0, 4, 6, 8
Z_WIDTH = SLOTS * PLANE + 128
SPLIT = 11
CHUNK = 4


def params(mib):
    return pltpu.CompilerParams(vmem_limit_bytes=mib * 2**20)


def lanes(rows, width):
    return lax.broadcasted_iota(jnp.int32, (rows, width), 1)


def last(side):
    return EDGE - 1 if side == 0 else 0


def roll(value, shift):
    width = value.shape[1]
    if isinstance(shift, int):
        shift = shift % width
        if shift == 0:
            return value
    return pltpu.roll(value, shift, 1)


def place():
    return lax.axis_index("gx") % 2, lax.axis_index("gz") % 2, lax.axis_index("gy")


def interior(block, wall, columns, write, first, stop, carry=None):
    lane = lanes(CIN, PLANE)
    z_of = lane % EDGE
    z_first, z_last = z_of == 0, z_of == EDGE - 1
    y_first, y_last = lane < EDGE, lane >= PLANE - EDGE
    zero = jnp.zeros((CIN, PLANE), BF)
    before, current = carry if carry is not None else (None, None)
    for x in range(first, stop):
        centre = block(x)
        z_less = jnp.where(z_first, zero, roll(centre, 1))
        z_more = jnp.where(z_last, zero, roll(centre, -1))
        buffer = x % 2
        for tap_z, value in enumerate((z_less, centre, z_more)):
            for tap_y in range(3):
                if tap_y == 0:
                    shifted = jnp.where(y_first, zero, roll(value, EDGE))
                elif tap_y == 1:
                    shifted = value
                else:
                    shifted = jnp.where(y_last, zero, roll(value, -EDGE))
                start = (tap_y * 3 + tap_z) * CIN
                columns[buffer, start : start + CIN, :] = shifted
        part = jnp.dot(wall[...], columns[buffer], preferred_element_type=F32)
        if x > 0:
            write(x - 1, before + part[2 * COUT :])
            before = current + part[COUT : 2 * COUT]
        else:
            before = part[COUT : 2 * COUT]
        current = part[:COUT]
    if stop == EDGE:
        write(EDGE - 1, before)
    return before, current


def write_plane(acc):
    def write(x, value):
        acc[:, x * PLANE : (x + 1) * PLANE] = value

    return write


def plane_of(block):
    return lambda x: block[:, x * PLANE : (x + 1) * PLANE]


def pack_and_convolve(blocks, weight, held, faces_y, faces_z, acc, carry, rest, wall, columns, first, weights, sems, weight_sem):
    width = VOX // CHUNK
    copies = []
    for slot in range(SLOTS):
        for part in range(CHUNK):
            at = pl.ds(part * width, width)
            copies.append(
                pltpu.make_async_copy(
                    blocks.at[slot, :, at], (first, held)[slot].at[:, at], sems.at[slot * CHUNK + part]
                )
            )
    weight_copy = pltpu.make_async_copy(weight, weights, weight_sem)
    copies[0].start()
    weight_copy.start()
    for copy in copies[1:]:
        copy.start()
    lane = lanes(CIN, PLANE)
    half_lane = lanes(CIN, 128)
    for slot in range(SLOTS):
        planes_z = [jnp.zeros((CIN, PLANE), BF)] * 2
        halves = [[jnp.zeros((CIN, 128), BF)] * 2 for _ in range(2)]
        for x in range(EDGE):
            if x % (EDGE // CHUNK) == 0:
                copies[slot * CHUNK + x // (EDGE // CHUNK)].wait()
            centre = (first, held)[slot][:, x * PLANE : (x + 1) * PLANE]
            moved = roll(centre, x)
            planes_z[0] = jnp.where(lane % EDGE == (x + EDGE - 1) % EDGE, moved, planes_z[0])
            planes_z[1] = jnp.where(lane % EDGE == x, moved, planes_z[1])
            ends = jnp.where(half_lane < 64, centre[:, :128], centre[:, 128:])
            moved = roll(ends, (x % 8) * EDGE)
            part = x // 8
            halves[0][part] = jnp.where(half_lane // EDGE == (x + 7) % 8, moved, halves[0][part])
            halves[1][part] = jnp.where(half_lane // EDGE == x % 8, moved, halves[1][part])
        faces_z[slot] = roll(planes_z[0], 1 - EDGE)
        faces_z[2 + slot] = planes_z[1]
        for part in range(2):
            at = slice(part * 128, (part + 1) * 128)
            faces_y[slot, :, at] = roll(halves[0][part], EDGE)
            faces_y[2 + slot, :, at] = halves[1][part]
        if slot == 0:
            weight_copy.wait()
            for tap_x in range(3):
                wall[tap_x * COUT : (tap_x + 1) * COUT, :] = weights[
                    :, tap_x * TAPS * CIN : (tap_x + 1) * TAPS * CIN
                ]
            before, current = interior(
                plane_of(first), wall, columns, write_plane(acc), 0, SPLIT
            )
            carry[0], carry[1] = before, current
            rest[...] = first[:, SPLIT * PLANE :]


def end_first(rest, wall, carry, tie, acc, columns):
    def block(x):
        return rest[:, (x - SPLIT) * PLANE : (x - SPLIT + 1) * PLANE]

    def write(x, value):
        x = x - (SPLIT - 1)
        acc[:, x * PLANE : (x + 1) * PLANE] = value

    interior(block, wall, columns, write, SPLIT, EDGE, (carry[0], carry[1]))


def pack_for_y(faces_y, far_a, far_b, out):
    parity, _, at_y = place()
    odd_x = parity == 1
    for slot in range(SLOTS):
        out[slot, :, :PLANE] = faces_y[at_y * 2 + slot]
        start = pl.multiple_of((1 - at_y) * 128, 128)
        a = far_a[slot, :, pl.ds(start, 128)]
        b = far_b[slot, :, pl.ds(start, 128)]
        out[slot, :, PLANE : PLANE + 128] = jnp.where(odd_x, a, b)
        out[slot, :, PLANE + 128 :] = jnp.where(odd_x, b, a)


def corner_lane(k):
    return k // 2 * EDGE + 6 + k % 2


def pack_for_z(faces_z, far_a, far_b, far_y, out_a, out_b):
    parity_x, parity_z, at_y = place()
    odd_x, odd_z = parity_x == 1, parity_z == 1
    lane = lanes(CIN, PLANE)
    half_lane = lanes(CIN, 128)
    row = at_y * 112
    packs = []
    for side in range(2):
        z = last(side)
        pack = jnp.zeros((CIN, PLANE), BF)
        corner = jnp.zeros((CIN, 128), BF)
        for slot in range(SLOTS):
            a, b = far_a[slot], far_b[slot]
            pair = (jnp.where(odd_x, a, b), jnp.where(odd_x, b, a))
            for d in range(2):
                k = d * 2 + slot
                pack = jnp.where(lane % EDGE == k, roll(pair[d], k - z), pack)
                edge = far_y[slot, :, PLANE + d * 128 : PLANE + (d + 1) * 128]
                target = corner_lane(k)
                moved = pltpu.roll(edge, (target - z - row + 128) % 128, 1)
                corner = jnp.where(half_lane == target, moved, corner)
            k = 4 + slot
            pack = jnp.where(lane % EDGE == k, roll(far_y[slot, :, :PLANE], k - z), pack)
        slim = jnp.where(half_lane % EDGE < 8, pack[:, :128], roll(pack[:, 128:], 8))
        packs.append(jnp.where((half_lane % 8 >= 6) & (half_lane % EDGE < 8), corner, slim))
    first, second = packs
    out_a[:, SLOTS * PLANE :] = jnp.where(odd_z, second, first)
    out_b[:, SLOTS * PLANE :] = jnp.where(odd_z, first, second)
    for slot in range(SLOTS):
        at = slice(slot * PLANE, (slot + 1) * PLANE)
        out_a[:, at] = faces_z[parity_z * 2 + slot]
        out_b[:, at] = faces_z[(1 - parity_z) * 2 + slot]


def pick(code, choices):
    result = choices[-1][1]
    for known, value in reversed(choices[:-1]):
        result = jnp.where(code == known, value, result)
    return result


def sign(side):
    return -1 if side == 0 else 1


def link(links, slot, dx, dy, dz):
    index = (dx + 1) * 9 + (dy + 1) * 3 + dz + 1
    value = links[slot, index if index < 13 else index - 1]
    clean = jnp.maximum(value, 0)
    return value >= 0, clean // 2, clean % 2


def whole(table, present, index):
    return jnp.where(present, table[index], jnp.zeros((CIN, PLANE), BF))


def column(table, present, index, source, side):
    target = 0 if side == 0 else EDGE - 1
    moved = pltpu.roll(table[index], (target - source + PLANE) % PLANE, 1)
    return jnp.where(present, moved, jnp.zeros((CIN, PLANE), BF))


def short(table, present, index, source, target):
    start = pl.multiple_of((source // 128) * 128, 128)
    value = table[index, :, pl.ds(start, 128)]
    moved = pltpu.roll(value, (target - source % 128 + 128) % 128, 1)
    return jnp.where(present, moved, jnp.zeros((CIN, 128), BF))


def put_corner(row, side, value):
    return jnp.where(lanes(CIN, 128) == (127 if side == 0 else EDGE), value, row)


def fill_columns(columns, buffer, centre, sides, rows):
    lane = lanes(CIN, PLANE)
    half_lane = lanes(CIN, 128)
    less = jnp.where(lane % EDGE == 0, sides[0], roll(centre, 1))
    more = jnp.where(lane % EDGE == EDGE - 1, sides[1], roll(centre, -1))
    for minor, value in enumerate((less, centre, more)):
        low, high = roll(rows[0], 1 - minor), roll(rows[1], 113 - minor)
        for major in range(3):
            start = (major * 3 + minor) * CIN
            at = slice(start, start + CIN)
            if major == 1:
                columns[buffer, at, :] = value
            elif major == 0:
                shifted = roll(value, EDGE)
                columns[buffer, at, :128] = jnp.where(half_lane < EDGE, low, shifted[:, :128])
                columns[buffer, at, 128:] = shifted[:, 128:]
            else:
                shifted = roll(value, -EDGE)
                columns[buffer, at, :128] = shifted[:, :128]
                columns[buffer, at, 128:] = jnp.where(half_lane >= 112, high, shifted[:, 128:])


def any_of(terms):
    result = terms[0]
    for term in terms[1:]:
        result = result | term
    return result


def near(links, slot, dx, dy, dz):
    present, code, _ = link(links, slot, dx, dy, dz)
    return present & (code < 4)


def add_rows(acc, sheet, side):
    half_o = lanes(COUT, 128)
    none = jnp.zeros((COUT, 128), F32)
    for x in range(EDGE):
        part = sheet[:, (x // 8) * 128 : (x // 8 + 1) * 128]
        if side == 0:
            moved = jnp.where(half_o < EDGE, roll(part, -(x % 8) * EDGE), none)
            at = slice(x * PLANE, x * PLANE + 128)
        else:
            moved = jnp.where(half_o >= 112, roll(part, 112 - (x % 8) * EDGE), none)
            at = slice(x * PLANE + 128, (x + 1) * PLANE)
        acc[:, at] = acc[:, at] + moved


def spread(sheet, side, x):
    lane_o = lanes(COUT, PLANE)
    moved = roll(sheet, last(1 - side) - x)
    return jnp.where(lane_o % EDGE == last(1 - side), moved, jnp.zeros((COUT, PLANE), F32))


def near_x(links, table, wall, columns, acc, slot, d):
    present, code, u = link(links, slot, sign(d), 0, 0)
    centre = whole(table, present, jnp.minimum(code, 1) * 4 + d * 2 + u)
    sides = []
    for f in range(2):
        present, code, u = link(links, slot, sign(d), 0, sign(f))
        index = jnp.minimum(code, 1) * 4 + d * 2 + u
        sides.append(column(table, present & (code < 4), index, last(f), f))
    rows = []
    for e in range(2):
        far = 112 if e == 0 else 0

        def index_of(code, u):
            return pick(
                code,
                (
                    (0, OWN_X + d * 2 + u),
                    (1, FAR_X + d * 2 + u),
                    (2, FAR_Y + u),
                    (3, EDGE_Y + d * 2 + u),
                ),
            )

        def start_of(code):
            return pick(
                code, ((0, last(e) * EDGE), (1, last(e) * EDGE), (2, last(d) * EDGE), (3, far))
            )

        present, code, u = link(links, slot, sign(d), sign(e), 0)
        row = short(table, present, index_of(code, u), start_of(code), 0)
        for f in range(2):
            present, code, u = link(links, slot, sign(d), sign(e), sign(f))
            target = 127 if f == 0 else EDGE
            source = start_of(code) + last(f)
            value = short(table, present & (code < 4), index_of(code, u), source, target)
            row = put_corner(row, f, value)
        rows.append(row)
    fill_columns(columns, d, centre, sides, rows)
    taps = wall[2 * d * COUT : (2 * d + 1) * COUT, :]
    x = last(1 - d)
    at = slice(x * PLANE, (x + 1) * PLANE)
    acc[:, at] = acc[:, at] + jnp.dot(taps, columns[d], preferred_element_type=F32)


def near_y(links, table, wall, columns, acc, slot, e):
    lane = lanes(CIN, PLANE)
    lane_o = lanes(COUT, PLANE)
    none = jnp.zeros((COUT, PLANE), F32)
    present, code, u = link(links, slot, 0, sign(e), 0)
    centre = whole(table, present, jnp.where(code == 0, OWN_Y + e * 2 + u, FAR_Y + u))
    sides = []
    for f in range(2):
        present, code, u = link(links, slot, 0, sign(e), sign(f))
        index = jnp.where(code == 0, OWN_Y + e * 2 + u, FAR_Y + u)
        sides.append(column(table, present & (code < 4), index, last(f), f))
    columns[e, :CIN, :] = jnp.where(lane % EDGE == 0, sides[0], roll(centre, 1))
    columns[e, CIN : 2 * CIN, :] = centre
    columns[e, 2 * CIN : 3 * CIN, :] = jnp.where(lane % EDGE == EDGE - 1, sides[1], roll(centre, -1))
    taps = wall[:, 2 * e * 3 * CIN : (2 * e + 1) * 3 * CIN]
    part = jnp.dot(taps, columns[e, : 3 * CIN, :], preferred_element_type=F32)
    sheet = part[COUT : 2 * COUT]
    sheet = sheet + jnp.where(lane_o < EDGE, none, roll(part[:COUT], EDGE))
    sheet = sheet + jnp.where(lane_o >= PLANE - EDGE, none, roll(part[2 * COUT :], -EDGE))
    add_rows(acc, sheet, e)


def near_z(links, faces_z, wall, columns, acc, slot, f):
    lane = lanes(CIN, PLANE)
    zero = jnp.zeros((CIN, PLANE), BF)
    lane_o = lanes(COUT, PLANE)
    none = jnp.zeros((COUT, PLANE), F32)
    _, _, u = link(links, slot, 0, 0, sign(f))
    centre = faces_z[f * 2 + u]
    columns[f, :CIN, :] = jnp.where(lane < EDGE, zero, roll(centre, EDGE))
    columns[f, CIN : 2 * CIN, :] = centre
    columns[f, 2 * CIN : 3 * CIN, :] = jnp.where(lane >= PLANE - EDGE, zero, roll(centre, -EDGE))
    taps = jnp.concatenate(
        [
            wall[:, (tap_y * 3 + 2 * f) * CIN : (tap_y * 3 + 2 * f + 1) * CIN]
            for tap_y in range(3)
        ],
        1,
    )
    part = jnp.dot(taps, columns[f, : 3 * CIN, :], preferred_element_type=F32)
    sheet = part[COUT : 2 * COUT]
    sheet = sheet + jnp.where(lane_o % EDGE == 0, none, roll(part[:COUT], 1))
    sheet = sheet + jnp.where(lane_o % EDGE == EDGE - 1, none, roll(part[2 * COUT :], -1))
    for x in range(EDGE):
        at = slice(x * PLANE, (x + 1) * PLANE)
        acc[:, at] = acc[:, at] + spread(sheet, f, x)


def finish_second(
    links_in, held, wall, tie, low_acc, high_acc, own_a, own_b, far_a, far_b, faces_y,
    far_y, faces_z, acc_a, acc_b, walls_z, columns, table, links, sem
):
    fetch = pltpu.make_async_copy(links_in, links, sem)
    fetch.start()
    parity_x, _, _ = place()
    odd_x = parity_x == 1
    for slot in range(SLOTS):
        a, b = own_a[slot], own_b[slot]
        table[OWN_X + slot] = jnp.where(odd_x, b, a)
        table[OWN_X + 2 + slot] = jnp.where(odd_x, a, b)
        a, b = far_a[slot], far_b[slot]
        table[FAR_X + slot] = jnp.where(odd_x, a, b)
        table[FAR_X + 2 + slot] = jnp.where(odd_x, b, a)
        table[FAR_Y + slot] = far_y[slot, :, :PLANE]
        for d in range(2):
            table[OWN_Y + d * 2 + slot] = faces_y[d * 2 + slot]
            table[EDGE_Y + d * 2 + slot, :, :128] = far_y[
                slot, :, PLANE + d * 128 : PLANE + (d + 1) * 128
            ]
            table[EDGE_Y + d * 2 + slot, :, 128:] = jnp.zeros((CIN, 128), BF)
    for x in range(EDGE):
        at = slice(x * PLANE, (x + 1) * PLANE)
        if x < SPLIT - 1:
            acc_a[:, at] = low_acc[:, at]
        else:
            source = x - (SPLIT - 1)
            acc_a[:, at] = high_acc[:, source * PLANE : (source + 1) * PLANE]
    interior(plane_of(held), wall, columns, write_plane(acc_b), 0, EDGE)
    for f in range(2):
        for tap_y in range(3):
            for tap_x in range(3):
                start = (tap_y * 3 + tap_x) * CIN
                source = (tap_y * 3 + 2 * f) * CIN
                walls_z[f, :, start : start + CIN] = wall[
                    tap_x * COUT : (tap_x + 1) * COUT, source : source + CIN
                ]
    fetch.wait()
    accs = (acc_a, acc_b)
    steps = (-1, 0, 1)
    for slot in range(SLOTS):
        acc = accs[slot]
        for d in range(2):
            wanted = any_of(
                [near(links, slot, sign(d), dy, dz) for dy in steps for dz in steps]
            )

            @pl.when(wanted)
            def _():
                near_x(links, table, wall, columns, acc, slot, d)

        for e in range(2):

            @pl.when(any_of([near(links, slot, 0, sign(e), dz) for dz in steps]))
            def _():
                near_y(links, table, wall, columns, acc, slot, e)

        for f in range(2):

            @pl.when(near(links, slot, 0, 0, sign(f)))
            def _():
                near_z(links, faces_z, wall, columns, acc, slot, f)


def far_z(links, table, walls_z, columns, slot, f):
    present, code, u = link(links, slot, 0, 0, sign(f))
    centre = whole(table, present & (code >= 4), FAR_Z + f * 2 + u)
    sides = []
    for d in range(2):
        present, code, u = link(links, slot, sign(d), 0, sign(f))
        index = jnp.where(code == 4, FAR_Z + f * 2 + u, EDGE_Z + f)
        source = jnp.where(code == 4, last(d), d * 2 + u)
        sides.append(column(table, present & (code >= 4), index, source, d))
    rows = []
    for e in range(2):
        present, code, u = link(links, slot, 0, sign(e), sign(f))
        index = jnp.where(code == 4, FAR_Z + f * 2 + u, TURN_Z + f)
        source = jnp.where(code == 4, last(e) * EDGE, (4 + u) * EDGE)
        row = short(table, present & (code >= 4), index, source, 0)
        for d in range(2):
            present, code, u = link(links, slot, sign(d), sign(e), sign(f))
            index = jnp.where(code == 4, FAR_Z + f * 2 + u, EDGE_Z + f)
            source = pick(
                code,
                (
                    (4, last(e) * EDGE + last(d)),
                    (5, last(e) * EDGE + d * 2 + u),
                    (6, last(d) * EDGE + 4 + u),
                    (7, d * EDGE + 6 + u),
                ),
            )
            target = 127 if d == 0 else EDGE
            value = short(table, present & (code >= 4), index, source, target)
            row = put_corner(row, d, value)
        rows.append(row)
    fill_columns(columns, f, centre, sides, rows)
    return jnp.dot(walls_z[f], columns[f], preferred_element_type=F32)


def upright(row):
    size = row.shape[1]
    across = lax.broadcasted_iota(jnp.int32, (size, size), 1)
    down = lax.broadcasted_iota(jnp.int32, (size, size), 0)
    wide = jnp.where(across == down, jnp.broadcast_to(row, (size, size)), 0.0)
    return jnp.sum(wide, axis=1, keepdims=True)


def finish(
    links_in, count_in, acc_a, acc_b, got_a, got_b, walls_z, bias_row, head, head_bias_row, turn,
    out_far, columns, table, sheets, out, links, count, sems, out_sems
):
    fetch_links = pltpu.make_async_copy(links_in, links, sems.at[0])
    fetch_count = pltpu.make_async_copy(count_in, count, sems.at[1])
    fetch_links.start()
    fetch_count.start()
    _, parity_z, _ = place()
    odd_z = parity_z == 1
    bias, head_bias = upright(bias_row[...]), upright(head_bias_row[...])
    weights = head[...]
    for slot in range(SLOTS):
        at = slice(slot * PLANE, (slot + 1) * PLANE)
        a, b = got_a[:, at], got_b[:, at]
        table[FAR_Z + slot] = jnp.where(odd_z, a, b)
        table[FAR_Z + 2 + slot] = jnp.where(odd_z, b, a)
    a, b = got_a[:, SLOTS * PLANE :], got_b[:, SLOTS * PLANE :]
    for f, value in enumerate((jnp.where(odd_z, a, b), jnp.where(odd_z, b, a))):
        table[EDGE_Z + f, :, :128] = value
        table[EDGE_Z + f, :, 128:] = roll(value, -8)
        table[TURN_Z + f] = jnp.dot(
            table[EDGE_Z + f], turn[...], preferred_element_type=F32
        ).astype(BF)
    fetch_links.wait()
    fetch_count.wait()
    accs = (acc_a, acc_b)
    steps = (-1, 0, 1)

    def emit(slot, total, x):
        hidden = jnp.maximum(total + bias, 0.0).astype(BF)
        mixed = jnp.dot(weights, hidden, preferred_element_type=F32) + head_bias
        out[slot, :, x * PLANE : (x + 1) * PLANE] = mixed.astype(BF)
        ship(slot, x)

    width = VOX // CHUNK

    def copy_out(slot, part):
        at = pl.ds(part * width, width)
        return pltpu.make_async_copy(
            out.at[slot, :, at], out_far.at[slot, :, at], out_sems.at[slot * CHUNK + part]
        )

    def ship(slot, x):
        if (x + 1) % (EDGE // CHUNK) == 0:
            copy_out(slot, x // (EDGE // CHUNK)).start()

    for slot in range(SLOTS):
        acc = accs[slot]
        wanted = []
        for f in range(2):
            terms = []
            for dx in steps:
                for dy in steps:
                    present, code, _ = link(links, slot, dx, dy, sign(f))
                    terms.append(present & (code >= 4))
            wanted.append(any_of(terms))
        used = slot < count[0, 0, 0]
        both = wanted[0] | wanted[1]

        @pl.when(used & both)
        def _():
            for f in range(2):

                @pl.when(wanted[f])
                def _():
                    sheets[f] = far_z(links, table, walls_z, columns, slot, f)

                @pl.when(jnp.logical_not(wanted[f]))
                def _():
                    sheets[f] = jnp.zeros((COUT, PLANE), F32)

            for x in range(EDGE):
                total = acc[:, x * PLANE : (x + 1) * PLANE]
                total = total + spread(sheets[0], 0, x) + spread(sheets[1], 1, x)
                emit(slot, total, x)

        @pl.when(used & jnp.logical_not(both))
        def _():
            for x in range(EDGE):
                emit(slot, acc[:, x * PLANE : (x + 1) * PLANE], x)

        @pl.when(jnp.logical_not(used))
        def _():
            for x in range(EDGE):
                out[slot, :, x * PLANE : (x + 1) * PLANE] = jnp.zeros((COUT, PLANE), BF)
                ship(slot, x)

    for slot in range(SLOTS):
        for part in range(CHUNK):
            copy_out(slot, part).wait()


VMEM = pl.BlockSpec(memory_space=pltpu.VMEM)
HBM = pl.BlockSpec(memory_space=pltpu.HBM)
ANY = pl.BlockSpec(memory_space=pl.ANY)


def shape(dims, kind=BF):
    return jax.ShapeDtypeStruct(dims, kind)


def in_hbm(value):
    return pltpu.with_memory_space_constraint(value, pltpu.HBM)


def swap(first, second, axis):
    length = lax.axis_size(axis)
    even = [(i, i ^ 1) for i in range(length)]
    odd = []
    for i in range(length):
        partner = ((i + 1) ^ 1) - 1
        for core in range(2):
            if 0 <= partner < length:
                odd.append((i * 2 + core, partner * 2 + core))
            else:
                odd.append((i * 2 + core, i * 2 + 1 - core))
    return lax.ppermute(first, axis, even), lax.ppermute(second, (axis, "gy"), odd)


def body(blocks, block_count, neighbours, conv_weight, conv_bias, head_weight, head_bias):
    volumes = blocks.reshape(SLOTS, CIN, VOX)
    links = neighbours.reshape(SLOTS, 26)
    odd_x = lax.axis_index("gx") % 2
    far_end = VOX - PLANE
    own_a = lax.dynamic_slice_in_dim(volumes, (1 - odd_x) * far_end, PLANE, 2)
    own_b = lax.dynamic_slice_in_dim(volumes, odd_x * far_end, PLANE, 2)
    far_a, far_b = swap(own_a, own_b, "gx")
    buffer = pltpu.VMEM((2, TAPS * CIN, PLANE), BF)
    block_flops = 2 * COUT * 27 * CIN * VOX
    held, faces_y, faces_z, low_acc, carry, rest, wall = pl.pallas_call(
        pack_and_convolve,
        out_shape=(
            shape((CIN, VOX)),
            shape((4, CIN, PLANE)),
            shape((4, CIN, PLANE)),
            shape((COUT, (SPLIT - 1) * PLANE), F32),
            shape((2, COUT, PLANE), F32),
            shape((CIN, (EDGE - SPLIT) * PLANE)),
            shape((3 * COUT, TAPS * CIN)),
        ),
        in_specs=[HBM, HBM],
        out_specs=(VMEM,) * 7,
        scratch_shapes=[
            buffer,
            pltpu.VMEM((CIN, VOX), BF),
            pltpu.VMEM((COUT, 27 * CIN), BF),
            pltpu.SemaphoreType.DMA((SLOTS * CHUNK,)),
            pltpu.SemaphoreType.DMA,
        ],
        compiler_params=params(16),
        cost_estimate=pl.CostEstimate(
            flops=2 * block_flops, bytes_accessed=4 * 2**20, transcendentals=0
        ),
    )(in_hbm(volumes), in_hbm(conv_weight))
    sent_y = pl.pallas_call(
        pack_for_y,
        out_shape=shape((SLOTS, CIN, 2 * PLANE)),
        in_specs=[VMEM, VMEM, VMEM],
        out_specs=VMEM,
        compiler_params=params(8),
    )(faces_y, far_a, far_b)
    far_y = lax.ppermute(sent_y, "gy", [(0, 1), (1, 0)])
    high_acc = pl.pallas_call(
        end_first,
        out_shape=shape((COUT, (EDGE - SPLIT + 1) * PLANE), F32),
        in_specs=[VMEM, VMEM, VMEM, ANY],
        out_specs=VMEM,
        scratch_shapes=[buffer],
        compiler_params=params(16),
        cost_estimate=pl.CostEstimate(
            flops=block_flops, bytes_accessed=2**20, transcendentals=0
        ),
    )(rest, wall, carry, sent_y)
    sent_a, sent_b = pl.pallas_call(
        pack_for_z,
        out_shape=(shape((CIN, Z_WIDTH)), shape((CIN, Z_WIDTH))),
        in_specs=[VMEM, VMEM, VMEM, VMEM],
        out_specs=(VMEM, VMEM),
        compiler_params=params(8),
    )(faces_z, far_a, far_b, far_y)
    got_a, got_b = swap(sent_a, sent_b, "gz")
    smem_links = pltpu.SMEM((SLOTS, 26), jnp.int32)
    acc_a, acc_b, walls_z = pl.pallas_call(
        finish_second,
        out_shape=(
            shape((COUT, VOX), F32), shape((COUT, VOX), F32), shape((2, COUT, TAPS * CIN))
        ),
        in_specs=[ANY, VMEM, VMEM, ANY] + [VMEM] * 9,
        out_specs=(VMEM,) * 3,
        scratch_shapes=[
            buffer,
            pltpu.VMEM((NEAR_SOURCES, CIN, PLANE), BF),
            smem_links,
            pltpu.SemaphoreType.DMA,
        ],
        compiler_params=params(16),
        cost_estimate=pl.CostEstimate(
            flops=2 * block_flops, bytes_accessed=2 * 2**20, transcendentals=0
        ),
    )(
        links, held, wall, sent_a, low_acc, high_acc, own_a, own_b, far_a, far_b, faces_y,
        far_y, faces_z,
    )
    index = jnp.arange(PLANE)
    turn = (index[:, None] == (index % EDGE * EDGE + index // EDGE)[None, :]).astype(BF)
    outputs = pl.pallas_call(
        finish,
        out_shape=shape((SLOTS, COUT, VOX)),
        in_specs=[ANY] * 2 + [VMEM] * 9,
        out_specs=HBM,
        scratch_shapes=[
            buffer,
            pltpu.VMEM((Z_SOURCES, CIN, PLANE), BF),
            pltpu.VMEM((2, COUT, PLANE), F32),
            pltpu.VMEM((SLOTS, COUT, VOX), BF),
            smem_links,
            pltpu.SMEM((1, 1, 1), jnp.int32),
            pltpu.SemaphoreType.DMA((2,)),
            pltpu.SemaphoreType.DMA((SLOTS * CHUNK,)),
        ],
        compiler_params=params(16),
    )(
        links, block_count, acc_a, acc_b, got_a, got_b, walls_z, conv_bias.reshape(1, COUT),
        head_weight, head_bias.reshape(1, COUT), turn,
    )
    return outputs.reshape(1, 1, SLOTS, COUT, VOX)


def solution(mesh):
    placed = (
        P("gx", "gz", "gy", None, None),
        P("gx", "gz", "gy"),
        P("gx", "gz", "gy", None),
        P(),
        P(),
        P(),
        P(),
    )
    return jax.shard_map(
        body, mesh=mesh, in_specs=placed, out_specs=P("gx", "gz", "gy", None, None), check_vma=False
    )
```

profile of v0, /device:TPU:100, one launch (start us, length us, event | category | flops | bytes accessed | tf_op | source)
XLA Modules:
  0.0 23.7 jit_solution(5454891385014975548)
XLA Ops:
  0.0 1.0 %dynamic-slice_bitcast_fusion = (bf16[2,96,256]{2,1,0:T(8,128)(2,1)S(1)}, bf16[2,96,256]{2,1,0:T(8,128)(2,1)S(1)}) fusion(bf16[1,1,2,96,4096]{4,3,2,1,0:T(8,128)(2,1)} %param.7, s32[]{:T(128)S(6)} %select_n.34, s32[]{:T(128)S(6)} %select_n.33), kind=kLoop, calls=%fused_computation.2 | loop fusion | bytes 393224 | tf_op jit(solution)/shard_map/dynamic_slice | solution.py:627
  1.0 1.7 %collective-permute-start = (bf16[2,96,256]{2,1,0:T(8,128)(2,1)S(1)}, bf16[2,96,256]{2,1,0:T(8,128)(2,1)S(1)}, u32[]{:S(2)}, u32[]{:S(2)}) collective-permute-start(bf16[2,96,256]{2,1,0:T(8,128)(2,1)S(1)} %get-tuple-element.30.own_a), channel_id=1, source_target_pairs={{0,16},{16,0},{32,48},{48,32},{64,80},{80,64},{96,112},{112,96},{1... | collective-permute-start | bytes 294920 | tf_op jit(solution)/shard_map/ppermute | solution.py:618
  2.6 2.2 %collective-permute-start.1 = (bf16[2,96,256]{2,1,0:T(8,128)(2,1)S(1)}, bf16[2,96,256]{2,1,0:T(8,128)(2,1)S(1)}, u32[]{:S(2)}, u32[]{:S(2)}) collective-permute-start(bf16[2,96,256]{2,1,0:T(8,128)(2,1)S(1)} %get-tuple-element.29.own_b), channel_id=1, source_target_pairs={{0,1},{1,0},{16,32},{17,33},{32,16},{33,17},{48,64},{49,65},{64,48... | collective-permute-start | bytes 294920 | tf_op jit(solution)/shard_map/ppermute | solution.py:618
  4.8 4.3 %shard_map.73 = (bf16[96,4096]{1,0:T(8,128)(2,1)S(1)}, bf16[4,96,256]{2,1,0:T(8,128)(2,1)S(1)}, bf16[4,96,256]{2,1,0:T(8,128)(2,1)S(1)}, f32[48,2560]{1,0:T(8,12...) custom-call(bf16[2,96,4096]{2,1,0:T(8,128)(2,1)} %bitcast.13, ...), custom_call_target="tpu_custom_call" | custom-call | flops 2038431744 | bytes 4194304 | tf_op jit(solution)/shard_map/pallas_call | solution.py:631
  9.1 0.0 collective-permute-done.far_a
  9.1 0.2 collective-permute-done.1.far_b
  9.4 0.1 collective-permute-start.2
  10.2 0.0 copy-start.1
  10.2 0.9 %shard_map.76.high_acc = f32[48,1536]{1,0:T(8,128)S(1)} custom-call(bf16[96,1280]{1,0:T(8,128)(2,1)S(1)} %get-tuple-element.23.rest, bf16[144,864]{1,0:T(8,128)(2,1)S(1)} %get-tuple-element.18.wall, f32[2,48,256]{2,1,0:T(8,128)S(1)} %get-tuple-element.24.carry, bf16[2,96,512]{2,1,0:T(8,128)(2,1)S(1)} %shard_map.74.tie), custom_call_target="tpu_custom_call" | custom-call | flops 1019215872 | bytes 1048576 | tf_op jit(solution)/shard_map/pallas_call | solution.py:664
  11.1 0.0 collective-permute-done.2.far_y
  11.1 0.4 %shard_map.75 = (bf16[96,640]{1,0:T(8,128)(2,1)S(1)}, bf16[96,640]{1,0:T(8,128)(2,1)S(1)}) custom-call(bf16[4,96,256]{2,1,0:T(8,128)(2,1)S(1)} %get-tuple-element.19.faces_z, bf16[2,96,256]{2,1,0:T(8,128)(2,1)S(1)} %collective-permute-done.far_a, bf16[2,96,256]{2,1,0:T(8,128)(2,1)S(1)} %collective-permute-done.1.far_b, ...), custom_call_target="tpu_custom_call" | custom-call | tf_op jit(solution)/shard_map/pallas_call | solution.py:675
  11.6 0.2 collective-permute-start.3
  11.8 4.0 %collective-permute-start.4 = (bf16[96,640]{1,0:T(8,128)(2,1)S(1)}, bf16[96,640]{1,0:T(8,128)(2,1)S(1)}, u32[]{:S(2)}, u32[]{:S(2)}) collective-permute-start(bf16[96,640]{1,0:T(8,128)(2,1)S(1)} %get-tuple-element.27), channel_id=1, source_target_pairs={{0,1},{1,0},{2,4},{3,5},{4,2},{5,3},{6,8},{7,9},{8,6},{9,7},{10,12... | collective-permute-start | bytes 368648 | tf_op jit(solution)/shard_map/ppermute | solution.py:618
  15.8 0.0 copy-done.1
  15.8 0.0 copy-start
  15.8 0.0 copy-start.2
  15.8 0.0 copy-start.3
  15.8 4.7 %shard_map.77 = (f32[48,4096]{1,0:T(8,128)S(1)}, f32[48,4096]{1,0:T(8,128)S(1)}, bf16[2,48,864]{2,1,0:T(8,128)(2,1)S(1)}) custom-call(s32[2,26]{1,0:T(2,128)S(1)} %bitcast.9, bf16[96,4096]{1,0:T(8,128)(2,1)S(1)} %get-tuple-element.17.held, bf16[144,864]{1,0:T(8,128)(2,1)S(1)} %get-tuple-element.18.wall, bf16[96,640]{1,0:T(8,128)(2,1)S(1)} %get-tuple-element.21.tie, ...), custom_call_target="tpu_custom_call" | custom-call | flops 2038431744 | bytes 2097152 | tf_op jit(solution)/shard_map/pallas_call | solution.py:684
  20.5 0.0 collective-permute-done.3.got_a
  20.5 0.0 collective-permute-done.4.got_b
  20.5 0.0 copy-done
  20.6 0.0 copy-done.2
  20.6 0.0 copy-done.3
  20.6 3.0 %shard_map.78 = bf16[2,48,4096]{2,1,0:T(8,128)(2,1)} custom-call(s32[2,26]{1,0:T(2,128)S(1)} %bitcast.10, s32[1,1,1]{2,1,0:T(1,128)S(6)} %copy.8.count_in, f32[48,4096]{1,0:T(8,128)S(1)} %get-tuple-element.25.acc_a, f32[48,4096]{1,0:T(8,128)S(1)} %get-tuple-element.26.acc_b, bf16[96,640]{1,0:T(8,128)(2,1)S(1)} %collective-permute-done.3.got_a, ...), custom_call_target="tpu_custom_call" | custom-call | tf_op jit(solution)/shard_map/pallas_call | solution.py:707
  (3 shorter events, 0.1 us)
Async XLA Ops:
  1.0 8.2 %collective-permute-start = (bf16[2,96,256]{2,1,0:T(8,128)(2,1)S(1)}, bf16[2,96,256]{2,1,0:T(8,128)(2,1)S(1)}, u32[]{:S(2)}, u32[]{:S(2)}) collective-permute-start(bf16[2,96,256]{2,1,0:T(8,128)(2,1)S(1)} %get-tuple-element.30.own_a), channel_id=1, source_target_pairs={{0,16},{16,0},{32,48},{48,32},{64,80},{80,64},{96,112},{112,96},{1... | collective-permute-start | bytes 294920 | tf_op jit(solution)/shard_map/ppermute | solution.py:618
  2.6 6.7 %collective-permute-start.1 = (bf16[2,96,256]{2,1,0:T(8,128)(2,1)S(1)}, bf16[2,96,256]{2,1,0:T(8,128)(2,1)S(1)}, u32[]{:S(2)}, u32[]{:S(2)}) collective-permute-start(bf16[2,96,256]{2,1,0:T(8,128)(2,1)S(1)} %get-tuple-element.29.own_b), channel_id=1, source_target_pairs={{0,1},{1,0},{16,32},{17,33},{32,16},{33,17},{48,64},{49,65},{64,48... | collective-permute-start | bytes 294920 | tf_op jit(solution)/shard_map/ppermute | solution.py:618
  9.4 1.8 %collective-permute-start.2 = (bf16[2,96,512]{2,1,0:T(8,128)(2,1)S(1)}, bf16[2,96,512]{2,1,0:T(8,128)(2,1)S(1)}, u32[]{:S(2)}, u32[]{:S(2)}) collective-permute-start(bf16[2,96,512]{2,1,0:T(8,128)(2,1)S(1)} %shard_map.74.tie), channel_id=1, source_target_pairs={{0,1},{1,0},{2,3},{3,2},{4,5},{5,4},{6,7},{7,6},{8,9},{9,8},{10,11... | collective-permute-start | bytes 589832 | tf_op jit(solution)/shard_map/ppermute | solution.py:663
  10.2 5.6 %copy-start.1 = (s32[1,1,2,26]{3,2,1,0:T(2,128)S(1)}, s32[1,1,2,26]{3,2,1,0:T(2,128)}, u32[]{:S(2)}) copy-start(s32[1,1,2,26]{3,2,1,0:T(2,128)} %param.9) | copy-start | bytes 628
  11.6 9.0 %collective-permute-start.3 = (bf16[96,640]{1,0:T(8,128)(2,1)S(1)}, bf16[96,640]{1,0:T(8,128)(2,1)S(1)}, u32[]{:S(2)}, u32[]{:S(2)}) collective-permute-start(bf16[96,640]{1,0:T(8,128)(2,1)S(1)} %get-tuple-element.21.tie), channel_id=1, source_target_pairs={{0,2},{2,0},{4,6},{6,4},{8,10},{10,8},{12,14},{14,12},{1,3},{3,1},... | collective-permute-start | bytes 368648 | tf_op jit(solution)/shard_map/ppermute | solution.py:618
  11.8 8.8 %collective-permute-start.4 = (bf16[96,640]{1,0:T(8,128)(2,1)S(1)}, bf16[96,640]{1,0:T(8,128)(2,1)S(1)}, u32[]{:S(2)}, u32[]{:S(2)}) collective-permute-start(bf16[96,640]{1,0:T(8,128)(2,1)S(1)} %get-tuple-element.27), channel_id=1, source_target_pairs={{0,1},{1,0},{2,4},{3,5},{4,2},{5,3},{6,8},{7,9},{8,6},{9,7},{10,12... | collective-permute-start | bytes 368648 | tf_op jit(solution)/shard_map/ppermute | solution.py:618
  15.8 4.8 %copy-start = (bf16[48,48]{1,0:T(8,128)(2,1)S(1)}, bf16[48,48]{1,0:T(8,128)(2,1)}, u32[]{:S(2)}) copy-start(bf16[48,48]{1,0:T(8,128)(2,1)} %head.1) | copy-start | bytes 13828
  15.8 4.8 %copy-start.2 = (f32[48]{0:T(128)S(1)}, f32[48]{0:T(128)}, u32[]{:S(2)}) copy-start(f32[48]{0:T(128)} %param.11) | copy-start | bytes 580
  15.8 4.8 %copy-start.3 = (f32[48]{0:T(128)S(1)}, f32[48]{0:T(128)}, u32[]{:S(2)}) copy-start(f32[48]{0:T(128)} %param.13) | copy-start | bytes 580
where the time goes:
time: 23.5 us; the launch traced here: 23.7 us
  Pallas kernels  13.4 us (57%)
  starting transfers between devices  8.14 us (35%)
  local copies, waits for them, and re-layouts  0.97 us (4%)
  between operations  0.94 us (4%)
    ppermute x2, starting transfers between devices, swap(): lax.ppermute(second, (axis, 'gy'), odd)  6.19 us
    pallas_call x1, Pallas kernels, body(): pl.pallas_call(finish_second, out_shape=(shape((COUT, VOX), F32), shape((...  4.72 us
    pallas_call x1, Pallas kernels, body(): pl.pallas_call(pack_and_convolve, out_shape=(shape((CIN, VOX)), shape((4,...  4.33 us
    pallas_call x1, Pallas kernels, body(): pl.pallas_call(finish, out_shape=shape((SLOTS, COUT, VOX)), in_specs=[ANY...  2.97 us
    ppermute x2, starting transfers between devices, swap(): lax.ppermute(first, axis, even)  1.86 us
    dynamic_slice x1, local copies, waits for them, and re-layouts, body(): own_b = lax.dynamic_slice_in_dim(volumes, odd_x * far_end, PLANE, 2)  0.95 us
    pallas_call x1, Pallas kernels, body(): pl.pallas_call(end_first, out_shape=shape((COUT, (EDGE - SPLIT + 1) * PLA...  0.95 us
  transfers between devices with their start and end apart: 5, of which 1 were waited for; matrix products, arithmetic and copies ran while one was open for 0% of the time, Pallas kernels for 42%

commit v1 on v0

--- a/solution.py
+++ b/solution.py
@@ -11,14 +11,13 @@
 PLANE = 256
 VOX = 4096
 SLOTS = 2
-TAPS = 9
 BF = jnp.bfloat16
 F32 = jnp.float32
 
 OWN_X, FAR_X, FAR_Y, OWN_Y, EDGE_Y, NEAR_SOURCES = 0, 4, 8, 10, 14, 18
 FAR_Z, EDGE_Z, TURN_Z, Z_SOURCES = 0, 4, 6, 8
 Z_WIDTH = SLOTS * PLANE + 128
-SPLIT = 11
+SPLIT = 12
 CHUNK = 4
 
 
@@ -47,37 +46,38 @@
     return lax.axis_index("gx") % 2, lax.axis_index("gz") % 2, lax.axis_index("gy")
 
 
-def interior(block, wall, columns, write, first, stop, carry=None):
+def interior(block, wall, write, first, stop, carry=None):
     lane = lanes(CIN, PLANE)
     z_of = lane % EDGE
     z_first, z_last = z_of == 0, z_of == EDGE - 1
-    y_first, y_last = lane < EDGE, lane >= PLANE - EDGE
     zero = jnp.zeros((CIN, PLANE), BF)
+    lane_o = lanes(COUT, PLANE)
+    y_first, y_last = lane_o < EDGE, lane_o >= PLANE - EDGE
+    none = jnp.zeros((COUT, PLANE), F32)
     before, current = carry if carry is not None else (None, None)
+
+    def join(parts):
+        less = jnp.where(y_first, none, roll(parts[0], EDGE))
+        more = jnp.where(y_last, none, roll(parts[2], -EDGE))
+        return parts[1] + less + more
+
     for x in range(first, stop):
         centre = block(x)
         z_less = jnp.where(z_first, zero, roll(centre, 1))
         z_more = jnp.where(z_last, zero, roll(centre, -1))
-        buffer = x % 2
-        for tap_z, value in enumerate((z_less, centre, z_more)):
-            for tap_y in range(3):
-                if tap_y == 0:
-                    shifted = jnp.where(y_first, zero, roll(value, EDGE))
-                elif tap_y == 1:
-                    shifted = value
-                else:
-                    shifted = jnp.where(y_last, zero, roll(value, -EDGE))
-                start = (tap_y * 3 + tap_z) * CIN
-                columns[buffer, start : start + CIN, :] = shifted
-        part = jnp.dot(wall[...], columns[buffer], preferred_element_type=F32)
+        stack = jnp.concatenate([z_less, centre, z_more], 0)
+        part = jnp.dot(wall[...], stack, preferred_element_type=F32)
+        taps = [
+            [part[(y * 3 + k) * COUT : (y * 3 + k + 1) * COUT] for k in range(3)] for y in range(3)
+        ]
         if x > 0:
-            write(x - 1, before + part[2 * COUT :])
-            before = current + part[COUT : 2 * COUT]
+            write(x - 1, join([before[y] + taps[y][2] for y in range(3)]))
+            before = [current[y] + taps[y][1] for y in range(3)]
         else:
-            before = part[COUT : 2 * COUT]
-        current = part[:COUT]
+            before = [taps[y][1] for y in range(3)]
+        current = [taps[y][0] for y in range(3)]
     if stop == EDGE:
-        write(EDGE - 1, before)
+        write(EDGE - 1, join(before))
     return before, current
 
 
@@ -92,7 +92,7 @@
     return lambda x: block[:, x * PLANE : (x + 1) * PLANE]
 
 
-def pack_and_convolve(blocks, weight, held, faces_y, faces_z, acc, carry, rest, wall, columns, first, weights, sems, weight_sem):
+def pack_and_convolve(blocks, weight, held, faces_y, faces_z, acc, carry, rest, wall, first, weights, sems, weight_sem):
     width = VOX // CHUNK
     copies = []
     for slot in range(SLOTS):
@@ -133,18 +133,20 @@
             faces_y[2 + slot, :, at] = halves[1][part]
         if slot == 0:
             weight_copy.wait()
-            for tap_x in range(3):
-                wall[tap_x * COUT : (tap_x + 1) * COUT, :] = weights[
-                    :, tap_x * TAPS * CIN : (tap_x + 1) * TAPS * CIN
-                ]
+            for tap_y in range(3):
+                for tap_x in range(3):
+                    row = (tap_y * 3 + tap_x) * COUT
+                    source = (tap_x * 3 + tap_y) * 3 * CIN
+                    wall[row : row + COUT, :] = weights[:, source : source + 3 * CIN]
             before, current = interior(
-                plane_of(first), wall, columns, write_plane(acc), 0, SPLIT
+                plane_of(first), wall, write_plane(acc), 0, SPLIT
             )
-            carry[0], carry[1] = before, current
+            for tap_y in range(3):
+                carry[tap_y], carry[3 + tap_y] = before[tap_y], current[tap_y]
             rest[...] = first[:, SPLIT * PLANE :]
 
 
-def end_first(rest, wall, carry, tie, acc, columns):
+def end_first(rest, wall, carry, tie, acc):
     def block(x):
         return rest[:, (x - SPLIT) * PLANE : (x - SPLIT + 1) * PLANE]
 
@@ -152,7 +154,9 @@
         x = x - (SPLIT - 1)
         acc[:, x * PLANE : (x + 1) * PLANE] = value
 
-    interior(block, wall, columns, write, SPLIT, EDGE, (carry[0], carry[1]))
+    before = [carry[k] for k in range(3)]
+    current = [carry[3 + k] for k in range(3)]
+    interior(block, wall, write, SPLIT, EDGE, (before, current))
 
 
 def pack_for_y(faces_y, far_a, far_b, out):
@@ -244,26 +248,36 @@
     return jnp.where(lanes(CIN, 128) == (127 if side == 0 else EDGE), value, row)
 
 
-def fill_columns(columns, buffer, centre, sides, rows):
+def shift_rows(part):
+    lane_o = lanes(COUT, PLANE)
+    none = jnp.zeros((COUT, PLANE), F32)
+    less = jnp.where(lane_o < EDGE, none, roll(part[:COUT], EDGE))
+    more = jnp.where(lane_o >= PLANE - EDGE, none, roll(part[2 * COUT :], -EDGE))
+    return part[COUT : 2 * COUT] + less + more
+
+
+def shift_lanes(part):
+    lane_o = lanes(COUT, PLANE)
+    none = jnp.zeros((COUT, PLANE), F32)
+    less = jnp.where(lane_o % EDGE == 0, none, roll(part[:COUT], 1))
+    more = jnp.where(lane_o % EDGE == EDGE - 1, none, roll(part[2 * COUT :], -1))
+    return part[COUT : 2 * COUT] + less + more
+
+
+def stack_lanes(centre, sides):
     lane = lanes(CIN, PLANE)
-    half_lane = lanes(CIN, 128)
     less = jnp.where(lane % EDGE == 0, sides[0], roll(centre, 1))
     more = jnp.where(lane % EDGE == EDGE - 1, sides[1], roll(centre, -1))
-    for minor, value in enumerate((less, centre, more)):
-        low, high = roll(rows[0], 1 - minor), roll(rows[1], 113 - minor)
-        for major in range(3):
-            start = (major * 3 + minor) * CIN
-            at = slice(start, start + CIN)
-            if major == 1:
-                columns[buffer, at, :] = value
-            elif major == 0:
-                shifted = roll(value, EDGE)
-                columns[buffer, at, :128] = jnp.where(half_lane < EDGE, low, shifted[:, :128])
-                columns[buffer, at, 128:] = shifted[:, 128:]
-            else:
-                shifted = roll(value, -EDGE)
-                columns[buffer, at, :128] = shifted[:, :128]
-                columns[buffer, at, 128:] = jnp.where(half_lane >= 112, high, shifted[:, 128:])
+    return jnp.concatenate([less, centre, more], 0)
+
+
+def row_share(taps, row, side):
+    stack = jnp.concatenate([roll(row, 1), row, roll(row, -1)], 0)
+    share = jnp.dot(taps, stack, preferred_element_type=F32)
+    half_o = lanes(COUT, 128)
+    if side == 0:
+        return jnp.where(half_o < EDGE, share, jnp.zeros((COUT, 128), F32))
+    return jnp.where(half_o >= 112, roll(share, 112), jnp.zeros((COUT, 128), F32))
 
 
 def any_of(terms):
@@ -298,7 +312,7 @@
     return jnp.where(lane_o % EDGE == last(1 - side), moved, jnp.zeros((COUT, PLANE), F32))
 
 
-def near_x(links, table, wall, columns, acc, slot, d):
+def near_x(links, table, wall, acc, slot, d):
     present, code, u = link(links, slot, sign(d), 0, 0)
     centre = whole(table, present, jnp.minimum(code, 1) * 4 + d * 2 + u)
     sides = []
@@ -306,7 +320,12 @@
         present, code, u = link(links, slot, sign(d), 0, sign(f))
         index = jnp.minimum(code, 1) * 4 + d * 2 + u
         sides.append(column(table, present & (code < 4), index, last(f), f))
-    rows = []
+    blocks_of = [slice((y * 3 + 2 * d) * COUT, (y * 3 + 2 * d + 1) * COUT) for y in range(3)]
+    taps = jnp.concatenate([wall[at, :] for at in blocks_of], 0)
+    part = jnp.dot(taps, stack_lanes(centre, sides), preferred_element_type=F32)
+    start = last(1 - d) * PLANE
+    at = slice(start, start + PLANE)
+    acc[:, at] = acc[:, at] + shift_rows(part)
     for e in range(2):
         far = 112 if e == 0 else 0
 
@@ -326,26 +345,21 @@
                 code, ((0, last(e) * EDGE), (1, last(e) * EDGE), (2, last(d) * EDGE), (3, far))
             )
 
-        present, code, u = link(links, slot, sign(d), sign(e), 0)
-        row = short(table, present, index_of(code, u), start_of(code), 0)
-        for f in range(2):
-            present, code, u = link(links, slot, sign(d), sign(e), sign(f))
-            target = 127 if f == 0 else EDGE
-            source = start_of(code) + last(f)
-            value = short(table, present & (code < 4), index_of(code, u), source, target)
-            row = put_corner(row, f, value)
-        rows.append(row)
-    fill_columns(columns, d, centre, sides, rows)
-    taps = wall[2 * d * COUT : (2 * d + 1) * COUT, :]
-    x = last(1 - d)
-    at = slice(x * PLANE, (x + 1) * PLANE)
-    acc[:, at] = acc[:, at] + jnp.dot(taps, columns[d], preferred_element_type=F32)
-
-
-def near_y(links, table, wall, columns, acc, slot, e):
-    lane = lanes(CIN, PLANE)
-    lane_o = lanes(COUT, PLANE)
-    none = jnp.zeros((COUT, PLANE), F32)
+        @pl.when(any_of([near(links, slot, sign(d), sign(e), dz) for dz in (-1, 0, 1)]))
+        def _():
+            present, code, u = link(links, slot, sign(d), sign(e), 0)
+            row = short(table, present, index_of(code, u), start_of(code), 0)
+            for f in range(2):
+                present, code, u = link(links, slot, sign(d), sign(e), sign(f))
+                target = 127 if f == 0 else EDGE
+                source = start_of(code) + last(f)
+                value = short(table, present & (code < 4), index_of(code, u), source, target)
+                row = put_corner(row, f, value)
+            half = slice(start + e * 128, start + (e + 1) * 128)
+            acc[:, half] = acc[:, half] + row_share(wall[blocks_of[2 * e], :], row, e)
+
+
+def near_y(links, table, wall, acc, slot, e):
     present, code, u = link(links, slot, 0, sign(e), 0)
     centre = whole(table, present, jnp.where(code == 0, OWN_Y + e * 2 + u, FAR_Y + u))
     sides = []
@@ -353,38 +367,27 @@
         present, code, u = link(links, slot, 0, sign(e), sign(f))
         index = jnp.where(code == 0, OWN_Y + e * 2 + u, FAR_Y + u)
         sides.append(column(table, present & (code < 4), index, last(f), f))
-    columns[e, :CIN, :] = jnp.where(lane % EDGE == 0, sides[0], roll(centre, 1))
-    columns[e, CIN : 2 * CIN, :] = centre
-    columns[e, 2 * CIN : 3 * CIN, :] = jnp.where(lane % EDGE == EDGE - 1, sides[1], roll(centre, -1))
-    taps = wall[:, 2 * e * 3 * CIN : (2 * e + 1) * 3 * CIN]
-    part = jnp.dot(taps, columns[e, : 3 * CIN, :], preferred_element_type=F32)
-    sheet = part[COUT : 2 * COUT]
-    sheet = sheet + jnp.where(lane_o < EDGE, none, roll(part[:COUT], EDGE))
-    sheet = sheet + jnp.where(lane_o >= PLANE - EDGE, none, roll(part[2 * COUT :], -EDGE))
-    add_rows(acc, sheet, e)
-
-
-def near_z(links, faces_z, wall, columns, acc, slot, f):
+    taps = wall[2 * e * 3 * COUT : (2 * e + 1) * 3 * COUT, :]
+    part = jnp.dot(taps, stack_lanes(centre, sides), preferred_element_type=F32)
+    add_rows(acc, shift_rows(part), e)
+
+
+def near_z(links, faces_z, wall, acc, slot, f):
     lane = lanes(CIN, PLANE)
     zero = jnp.zeros((CIN, PLANE), BF)
-    lane_o = lanes(COUT, PLANE)
-    none = jnp.zeros((COUT, PLANE), F32)
     _, _, u = link(links, slot, 0, 0, sign(f))
     centre = faces_z[f * 2 + u]
-    columns[f, :CIN, :] = jnp.where(lane < EDGE, zero, roll(centre, EDGE))
-    columns[f, CIN : 2 * CIN, :] = centre
-    columns[f, 2 * CIN : 3 * CIN, :] = jnp.where(lane >= PLANE - EDGE, zero, roll(centre, -EDGE))
+    less = jnp.where(lane < EDGE, zero, roll(centre, EDGE))
+    more = jnp.where(lane >= PLANE - EDGE, zero, roll(centre, -EDGE))
     taps = jnp.concatenate(
         [
-            wall[:, (tap_y * 3 + 2 * f) * CIN : (tap_y * 3 + 2 * f + 1) * CIN]
+            wall[tap_y * 3 * COUT : (tap_y + 1) * 3 * COUT, 2 * f * CIN : (2 * f + 1) * CIN]
             for tap_y in range(3)
         ],
         1,
     )
-    part = jnp.dot(taps, columns[f, : 3 * CIN, :], preferred_element_type=F32)
-    sheet = part[COUT : 2 * COUT]
-    sheet = sheet + jnp.where(lane_o % EDGE == 0, none, roll(part[:COUT], 1))
-    sheet = sheet + jnp.where(lane_o % EDGE == EDGE - 1, none, roll(part[2 * COUT :], -1))
+    stack = jnp.concatenate([less, centre, more], 0)
+    sheet = shift_lanes(jnp.dot(taps, stack, preferred_element_type=F32))
     for x in range(EDGE):
         at = slice(x * PLANE, (x + 1) * PLANE)
         acc[:, at] = acc[:, at] + spread(sheet, f, x)
@@ -392,7 +395,7 @@
 
 def finish_second(
     links_in, held, wall, tie, low_acc, high_acc, own_a, own_b, far_a, far_b, faces_y,
-    far_y, faces_z, acc_a, acc_b, walls_z, columns, table, links, sem
+    far_y, faces_z, acc_a, acc_b, walls_z, table, links, sem
 ):
     fetch = pltpu.make_async_copy(links_in, links, sem)
     fetch.start()
@@ -419,15 +422,14 @@
         else:
             source = x - (SPLIT - 1)
             acc_a[:, at] = high_acc[:, source * PLANE : (source + 1) * PLANE]
-    interior(plane_of(held), wall, columns, write_plane(acc_b), 0, EDGE)
+    interior(plane_of(held), wall, write_plane(acc_b), 0, EDGE)
     for f in range(2):
         for tap_y in range(3):
             for tap_x in range(3):
-                start = (tap_y * 3 + tap_x) * CIN
-                source = (tap_y * 3 + 2 * f) * CIN
-                walls_z[f, :, start : start + CIN] = wall[
-                    tap_x * COUT : (tap_x + 1) * COUT, source : source + CIN
-                ]
+                row = (tap_y * 3 + tap_x) * COUT
+                walls_z[
+                    f, tap_y * COUT : (tap_y + 1) * COUT, tap_x * CIN : (tap_x + 1) * CIN
+                ] = wall[row : row + COUT, 2 * f * CIN : (2 * f + 1) * CIN]
     fetch.wait()
     accs = (acc_a, acc_b)
     steps = (-1, 0, 1)
@@ -440,22 +442,22 @@
 
             @pl.when(wanted)
             def _():
-                near_x(links, table, wall, columns, acc, slot, d)
+                near_x(links, table, wall, acc, slot, d)
 
         for e in range(2):
 
             @pl.when(any_of([near(links, slot, 0, sign(e), dz) for dz in steps]))
             def _():
-                near_y(links, table, wall, columns, acc, slot, e)
+                near_y(links, table, wall, acc, slot, e)
 
         for f in range(2):
 
             @pl.when(near(links, slot, 0, 0, sign(f)))
             def _():
-                near_z(links, faces_z, wall, columns, acc, slot, f)
-
-
-def far_z(links, table, walls_z, columns, slot, f):
+                near_z(links, faces_z, wall, acc, slot, f)
+
+
+def far_z(links, table, walls_z, sheets, slot, f):
     present, code, u = link(links, slot, 0, 0, sign(f))
     centre = whole(table, present & (code >= 4), FAR_Z + f * 2 + u)
     sides = []
@@ -464,30 +466,38 @@
         index = jnp.where(code == 4, FAR_Z + f * 2 + u, EDGE_Z + f)
         source = jnp.where(code == 4, last(d), d * 2 + u)
         sides.append(column(table, present & (code >= 4), index, source, d))
-    rows = []
+    part = jnp.dot(walls_z[f], stack_lanes(centre, sides), preferred_element_type=F32)
+    sheets[f] = shift_rows(part)
     for e in range(2):
-        present, code, u = link(links, slot, 0, sign(e), sign(f))
-        index = jnp.where(code == 4, FAR_Z + f * 2 + u, TURN_Z + f)
-        source = jnp.where(code == 4, last(e) * EDGE, (4 + u) * EDGE)
-        row = short(table, present & (code >= 4), index, source, 0)
-        for d in range(2):
-            present, code, u = link(links, slot, sign(d), sign(e), sign(f))
-            index = jnp.where(code == 4, FAR_Z + f * 2 + u, EDGE_Z + f)
-            source = pick(
-                code,
-                (
-                    (4, last(e) * EDGE + last(d)),
-                    (5, last(e) * EDGE + d * 2 + u),
-                    (6, last(d) * EDGE + 4 + u),
-                    (7, d * EDGE + 6 + u),
-                ),
-            )
-            target = 127 if d == 0 else EDGE
-            value = short(table, present & (code >= 4), index, source, target)
-            row = put_corner(row, d, value)
-        rows.append(row)
-    fill_columns(columns, f, centre, sides, rows)
-    return jnp.dot(walls_z[f], columns[f], preferred_element_type=F32)
+        terms = []
+        for dx in (-1, 0, 1):
+            present, code, _ = link(links, slot, dx, sign(e), sign(f))
+            terms.append(present & (code >= 4))
+
+        @pl.when(any_of(terms))
+        def _():
+            present, code, u = link(links, slot, 0, sign(e), sign(f))
+            index = jnp.where(code == 4, FAR_Z + f * 2 + u, TURN_Z + f)
+            source = jnp.where(code == 4, last(e) * EDGE, (4 + u) * EDGE)
+            row = short(table, present & (code >= 4), index, source, 0)
+            for d in range(2):
+                present, code, u = link(links, slot, sign(d), sign(e), sign(f))
+                index = jnp.where(code == 4, FAR_Z + f * 2 + u, EDGE_Z + f)
+                source = pick(
+                    code,
+                    (
+                        (4, last(e) * EDGE + last(d)),
+                        (5, last(e) * EDGE + d * 2 + u),
+                        (6, last(d) * EDGE + 4 + u),
+                        (7, d * EDGE + 6 + u),
+                    ),
+                )
+                target = 127 if d == 0 else EDGE
+                value = short(table, present & (code >= 4), index, source, target)
+                row = put_corner(row, d, value)
+            half = slice(e * 128, (e + 1) * 128)
+            taps = walls_z[f, 2 * e * COUT : (2 * e + 1) * COUT, :]
+            sheets[f, :, half] = sheets[f, :, half] + row_share(taps, row, e)
 
 
 def upright(row):
@@ -500,7 +510,7 @@
 
 def finish(
     links_in, count_in, acc_a, acc_b, got_a, got_b, walls_z, bias_row, head, head_bias_row, turn,
-    out_far, columns, table, sheets, out, links, count, sems, out_sems
+    out_far, table, sheets, out, links, count, sems, out_sems
 ):
     fetch_links = pltpu.make_async_copy(links_in, links, sems.at[0])
     fetch_count = pltpu.make_async_copy(count_in, count, sems.at[1])
@@ -564,16 +574,23 @@
 
                 @pl.when(wanted[f])
                 def _():
-                    sheets[f] = far_z(links, table, walls_z, columns, slot, f)
-
-                @pl.when(jnp.logical_not(wanted[f]))
+                    far_z(links, table, walls_z, sheets, slot, f)
+
+            for f in range(2):
+
+                @pl.when(wanted[f] & jnp.logical_not(wanted[1 - f]))
                 def _():
-                    sheets[f] = jnp.zeros((COUT, PLANE), F32)
-
-            for x in range(EDGE):
-                total = acc[:, x * PLANE : (x + 1) * PLANE]
-                total = total + spread(sheets[0], 0, x) + spread(sheets[1], 1, x)
-                emit(slot, total, x)
+                    sheet = sheets[f]
+                    for x in range(EDGE):
+                        total = acc[:, x * PLANE : (x + 1) * PLANE]
+                        emit(slot, total + spread(sheet, f, x), x)
+
+            @pl.when(wanted[0] & wanted[1])
+            def _():
+                for x in range(EDGE):
+                    total = acc[:, x * PLANE : (x + 1) * PLANE]
+                    total = total + spread(sheets[0], 0, x) + spread(sheets[1], 1, x)
+                    emit(slot, total, x)
 
         @pl.when(used & jnp.logical_not(both))
         def _():
@@ -626,7 +643,6 @@
     own_a = lax.dynamic_slice_in_dim(volumes, (1 - odd_x) * far_end, PLANE, 2)
     own_b = lax.dynamic_slice_in_dim(volumes, odd_x * far_end, PLANE, 2)
     far_a, far_b = swap(own_a, own_b, "gx")
-    buffer = pltpu.VMEM((2, TAPS * CIN, PLANE), BF)
     block_flops = 2 * COUT * 27 * CIN * VOX
     held, faces_y, faces_z, low_acc, carry, rest, wall = pl.pallas_call(
         pack_and_convolve,
@@ -635,14 +651,13 @@
             shape((4, CIN, PLANE)),
             shape((4, CIN, PLANE)),
             shape((COUT, (SPLIT - 1) * PLANE), F32),
-            shape((2, COUT, PLANE), F32),
+            shape((6, COUT, PLANE), F32),
             shape((CIN, (EDGE - SPLIT) * PLANE)),
-            shape((3 * COUT, TAPS * CIN)),
+            shape((9 * COUT, 3 * CIN)),
         ),
         in_specs=[HBM, HBM],
         out_specs=(VMEM,) * 7,
         scratch_shapes=[
-            buffer,
             pltpu.VMEM((CIN, VOX), BF),
             pltpu.VMEM((COUT, 27 * CIN), BF),
             pltpu.SemaphoreType.DMA((SLOTS * CHUNK,)),
@@ -666,7 +681,6 @@
         out_shape=shape((COUT, (EDGE - SPLIT + 1) * PLANE), F32),
         in_specs=[VMEM, VMEM, VMEM, ANY],
         out_specs=VMEM,
-        scratch_shapes=[buffer],
         compiler_params=params(16),
         cost_estimate=pl.CostEstimate(
             flops=block_flops, bytes_accessed=2**20, transcendentals=0
@@ -684,12 +698,11 @@
     acc_a, acc_b, walls_z = pl.pallas_call(
         finish_second,
         out_shape=(
-            shape((COUT, VOX), F32), shape((COUT, VOX), F32), shape((2, COUT, TAPS * CIN))
+            shape((COUT, VOX), F32), shape((COUT, VOX), F32), shape((2, 3 * COUT, 3 * CIN))
         ),
         in_specs=[ANY, VMEM, VMEM, ANY] + [VMEM] * 9,
         out_specs=(VMEM,) * 3,
         scratch_shapes=[
-            buffer,
             pltpu.VMEM((NEAR_SOURCES, CIN, PLANE), BF),
             smem_links,
             pltpu.SemaphoreType.DMA,
@@ -710,7 +723,6 @@
         in_specs=[ANY] * 2 + [VMEM] * 9,
         out_specs=HBM,
         scratch_shapes=[
-            buffer,
             pltpu.VMEM((Z_SOURCES, CIN, PLANE), BF),
             pltpu.VMEM((2, COUT, PLANE), F32),
             pltpu.VMEM((SLOTS, COUT, VOX), BF),

time: 23.5 us -> 23.5 us (level)
  the two profiles are of different devices: /device:TPU:100 before, /device:TPU:101 now
where the time goes in v1:
time: 23.5 us; the launch traced here: 23.9 us
  Pallas kernels  13.2 us (56%)
  starting transfers between devices  8.79 us (37%)
  local copies, waits for them, and re-layouts  0.97 us (4%)
  between operations  0.95 us (4%)
    pallas_call x1, Pallas kernels, body(): pl.pallas_call(finish_second, out_shape=(shape((COUT, VOX), F32), shape((...  5.91 us
    ppermute x2, starting transfers between devices, swap(): lax.ppermute(second, (axis, 'gy'), odd)  5.45 us
    pallas_call x1, Pallas kernels, body(): pl.pallas_call(pack_and_convolve, out_shape=(shape((CIN, VOX)), shape((4,...  3.98 us
    pallas_call x1, Pallas kernels, body(): pl.pallas_call(finish, out_shape=shape((SLOTS, COUT, VOX)), in_specs=[ANY...  2.08 us
    ppermute x1, starting transfers between devices, body(): far_y = lax.ppermute(sent_y, 'gy', [(0, 1), (1, 0)])  1.87 us
    ppermute x2, starting transfers between devices, swap(): lax.ppermute(first, axis, even)  1.47 us
    dynamic_slice x1, local copies, waits for them, and re-layouts, body(): own_b = lax.dynamic_slice_in_dim(volumes, odd_x * far_end, PLANE, 2)  0.95 us
    pallas_call x1, Pallas kernels, body(): pl.pallas_call(end_first, out_shape=shape((COUT, (EDGE - SPLIT + 1) * PLA...  0.76 us
  transfers between devices with their start and end apart: 5, of which 0 were waited for; matrix products, arithmetic and copies ran while one was open for 0% of the time, Pallas kernels for 45%

profile of v1, /device:TPU:101, one launch (start us, length us, event | category | flops | bytes accessed | tf_op | source)
XLA Modules:
  0.0 23.9 jit_solution(9240533858950651701)
XLA Ops:
  0.0 1.0 %dynamic-slice_bitcast_fusion = (bf16[2,96,256]{2,1,0:T(8,128)(2,1)S(1)}, bf16[2,96,256]{2,1,0:T(8,128)(2,1)S(1)}) fusion(bf16[1,1,2,96,4096]{4,3,2,1,0:T(8,128)(2,1)} %param.7, s32[]{:T(128)S(6)} %select_n.34, s32[]{:T(128)S(6)} %select_n.33), kind=kLoop, calls=%fused_computation.2 | loop fusion | bytes 393224 | tf_op jit(solution)/shard_map/dynamic_slice | solution.py:644
  1.0 1.4 %collective-permute-start = (bf16[2,96,256]{2,1,0:T(8,128)(2,1)S(1)}, bf16[2,96,256]{2,1,0:T(8,128)(2,1)S(1)}, u32[]{:S(2)}, u32[]{:S(2)}) collective-permute-start(bf16[2,96,256]{2,1,0:T(8,128)(2,1)S(1)} %get-tuple-element.30.own_a), channel_id=1, source_target_pairs={{0,16},{16,0},{32,48},{48,32},{64,80},{80,64},{96,112},{112,96},{1... | collective-permute-start | bytes 294920 | tf_op jit(solution)/shard_map/ppermute | solution.py:635
  2.3 1.9 %collective-permute-start.1 = (bf16[2,96,256]{2,1,0:T(8,128)(2,1)S(1)}, bf16[2,96,256]{2,1,0:T(8,128)(2,1)S(1)}, u32[]{:S(2)}, u32[]{:S(2)}) collective-permute-start(bf16[2,96,256]{2,1,0:T(8,128)(2,1)S(1)} %get-tuple-element.29.own_b), channel_id=1, source_target_pairs={{0,1},{1,0},{16,32},{17,33},{32,16},{33,17},{48,64},{49,65},{64,48... | collective-permute-start | bytes 294920 | tf_op jit(solution)/shard_map/ppermute | solution.py:635
  4.2 4.0 %shard_map.73 = (bf16[96,4096]{1,0:T(8,128)(2,1)S(1)}, bf16[4,96,256]{2,1,0:T(8,128)(2,1)S(1)}, bf16[4,96,256]{2,1,0:T(8,128)(2,1)S(1)}, f32[48,2816]{1,0:T(8,12...) custom-call(bf16[2,96,4096]{2,1,0:T(8,128)(2,1)} %bitcast.13, ...), custom_call_target="tpu_custom_call" | custom-call | flops 2038431744 | bytes 4194304 | tf_op jit(solution)/shard_map/pallas_call | solution.py:647
  8.2 0.0 collective-permute-done.far_a
  8.2 0.0 collective-permute-done.1.far_b
  8.3 1.9 %collective-permute-start.2 = (bf16[2,96,512]{2,1,0:T(8,128)(2,1)S(1)}, bf16[2,96,512]{2,1,0:T(8,128)(2,1)S(1)}, u32[]{:S(2)}, u32[]{:S(2)}) collective-permute-start(bf16[2,96,512]{2,1,0:T(8,128)(2,1)S(1)} %shard_map.74.tie), channel_id=1, source_target_pairs={{0,1},{1,0},{2,3},{3,2},{4,5},{5,4},{6,7},{7,6},{8,9},{9,8},{10,11... | collective-permute-start | bytes 589832 | tf_op jit(solution)/shard_map/ppermute | solution.py:678
  10.8 0.0 copy-start.1
  10.8 0.8 %shard_map.76.high_acc = f32[48,1280]{1,0:T(8,128)S(1)} custom-call(bf16[96,1024]{1,0:T(8,128)(2,1)S(1)} %get-tuple-element.23.rest, bf16[432,288]{1,0:T(8,128)(2,1)S(1)} %get-tuple-element.18.wall, f32[6,48,256]{2,1,0:T(8,128)S(1)} %get-tuple-element.24.carry, bf16[2,96,512]{2,1,0:T(8,128)(2,1)S(1)} %shard_map.74.tie), custom_call_target="tpu_custom_call" | custom-call | flops 1019215872 | bytes 1048576 | tf_op jit(solution)/shard_map/pallas_call | solution.py:679
  11.6 0.0 collective-permute-done.2.far_y
  11.6 0.4 %shard_map.75 = (bf16[96,640]{1,0:T(8,128)(2,1)S(1)}, bf16[96,640]{1,0:T(8,128)(2,1)S(1)}) custom-call(bf16[4,96,256]{2,1,0:T(8,128)(2,1)S(1)} %get-tuple-element.19.faces_z, bf16[2,96,256]{2,1,0:T(8,128)(2,1)S(1)} %collective-permute-done.far_a, bf16[2,96,256]{2,1,0:T(8,128)(2,1)S(1)} %collective-permute-done.1.far_b, ...), custom_call_target="tpu_custom_call" | custom-call | tf_op jit(solution)/shard_map/pallas_call | solution.py:689
  12.0 0.1 collective-permute-start.3
  12.1 3.6 %collective-permute-start.4 = (bf16[96,640]{1,0:T(8,128)(2,1)S(1)}, bf16[96,640]{1,0:T(8,128)(2,1)S(1)}, u32[]{:S(2)}, u32[]{:S(2)}) collective-permute-start(bf16[96,640]{1,0:T(8,128)(2,1)S(1)} %get-tuple-element.27), channel_id=1, source_target_pairs={{0,1},{1,0},{2,4},{3,5},{4,2},{5,3},{6,8},{7,9},{8,6},{9,7},{10,12... | collective-permute-start | bytes 368648 | tf_op jit(solution)/shard_map/ppermute | solution.py:635
  15.7 0.0 copy-done.1
  15.7 0.0 copy-start
  15.7 0.0 copy-start.2
  15.7 0.0 copy-start.3
  15.7 5.9 %shard_map.77 = (f32[48,4096]{1,0:T(8,128)S(1)}, f32[48,4096]{1,0:T(8,128)S(1)}, bf16[2,144,288]{2,1,0:T(8,128)(2,1)S(1)}) custom-call(s32[2,26]{1,0:T(2,128)S(1)} %bitcast.9, bf16[96,4096]{1,0:T(8,128)(2,1)S(1)} %get-tuple-element.17.held, bf16[432,288]{1,0:T(8,128)(2,1)S(1)} %get-tuple-element.18.wall, bf16[96,640]{1,0:T(8,128)(2,1)S(1)} %get-tuple-element.21.tie, ...), custom_call_target="tpu_custom_call" | custom-call | flops 2038431744 | bytes 2097152 | tf_op jit(solution)/shard_map/pallas_call | solution.py:698
  21.6 0.0 collective-permute-done.3.got_a
  21.6 0.0 collective-permute-done.4.got_b
  21.7 0.0 copy-done
  21.7 0.0 copy-done.2
  21.7 0.0 copy-done.3
  21.7 2.1 %shard_map.78 = bf16[2,48,4096]{2,1,0:T(8,128)(2,1)} custom-call(s32[2,26]{1,0:T(2,128)S(1)} %bitcast.10, s32[1,1,1]{2,1,0:T(1,128)S(6)} %copy.8.count_in, f32[48,4096]{1,0:T(8,128)S(1)} %get-tuple-element.25.acc_a, f32[48,4096]{1,0:T(8,128)S(1)} %get-tuple-element.26.acc_b, bf16[96,640]{1,0:T(8,128)(2,1)S(1)} %collective-permute-done.3.got_a, ...), custom_call_target="tpu_custom_call" | custom-call | tf_op jit(solution)/shard_map/pallas_call | solution.py:720
  (3 shorter events, 0.1 us)
Async XLA Ops:
  1.0 7.3 %collective-permute-start = (bf16[2,96,256]{2,1,0:T(8,128)(2,1)S(1)}, bf16[2,96,256]{2,1,0:T(8,128)(2,1)S(1)}, u32[]{:S(2)}, u32[]{:S(2)}) collective-permute-start(bf16[2,96,256]{2,1,0:T(8,128)(2,1)S(1)} %get-tuple-element.30.own_a), channel_id=1, source_target_pairs={{0,16},{16,0},{32,48},{48,32},{64,80},{80,64},{96,112},{112,96},{1... | collective-permute-start | bytes 294920 | tf_op jit(solution)/shard_map/ppermute | solution.py:635
  2.3 5.9 %collective-permute-start.1 = (bf16[2,96,256]{2,1,0:T(8,128)(2,1)S(1)}, bf16[2,96,256]{2,1,0:T(8,128)(2,1)S(1)}, u32[]{:S(2)}, u32[]{:S(2)}) collective-permute-start(bf16[2,96,256]{2,1,0:T(8,128)(2,1)S(1)} %get-tuple-element.29.own_b), channel_id=1, source_target_pairs={{0,1},{1,0},{16,32},{17,33},{32,16},{33,17},{48,64},{49,65},{64,48... | collective-permute-start | bytes 294920 | tf_op jit(solution)/shard_map/ppermute | solution.py:635
  8.3 3.3 %collective-permute-start.2 = (bf16[2,96,512]{2,1,0:T(8,128)(2,1)S(1)}, bf16[2,96,512]{2,1,0:T(8,128)(2,1)S(1)}, u32[]{:S(2)}, u32[]{:S(2)}) collective-permute-start(bf16[2,96,512]{2,1,0:T(8,128)(2,1)S(1)} %shard_map.74.tie), channel_id=1, source_target_pairs={{0,1},{1,0},{2,3},{3,2},{4,5},{5,4},{6,7},{7,6},{8,9},{9,8},{10,11... | collective-permute-start | bytes 589832 | tf_op jit(solution)/shard_map/ppermute | solution.py:678
  10.8 4.9 %copy-start.1 = (s32[1,1,2,26]{3,2,1,0:T(2,128)S(1)}, s32[1,1,2,26]{3,2,1,0:T(2,128)}, u32[]{:S(2)}) copy-start(s32[1,1,2,26]{3,2,1,0:T(2,128)} %param.9) | copy-start | bytes 628
  12.0 9.6 %collective-permute-start.3 = (bf16[96,640]{1,0:T(8,128)(2,1)S(1)}, bf16[96,640]{1,0:T(8,128)(2,1)S(1)}, u32[]{:S(2)}, u32[]{:S(2)}) collective-permute-start(bf16[96,640]{1,0:T(8,128)(2,1)S(1)} %get-tuple-element.21.tie), channel_id=1, source_target_pairs={{0,2},{2,0},{4,6},{6,4},{8,10},{10,8},{12,14},{14,12},{1,3},{3,1},... | collective-permute-start | bytes 368648 | tf_op jit(solution)/shard_map/ppermute | solution.py:635
  12.1 9.5 %collective-permute-start.4 = (bf16[96,640]{1,0:T(8,128)(2,1)S(1)}, bf16[96,640]{1,0:T(8,128)(2,1)S(1)}, u32[]{:S(2)}, u32[]{:S(2)}) collective-permute-start(bf16[96,640]{1,0:T(8,128)(2,1)S(1)} %get-tuple-element.27), channel_id=1, source_target_pairs={{0,1},{1,0},{2,4},{3,5},{4,2},{5,3},{6,8},{7,9},{8,6},{9,7},{10,12... | collective-permute-start | bytes 368648 | tf_op jit(solution)/shard_map/ppermute | solution.py:635
  15.7 6.0 %copy-start = (bf16[48,48]{1,0:T(8,128)(2,1)S(1)}, bf16[48,48]{1,0:T(8,128)(2,1)}, u32[]{:S(2)}) copy-start(bf16[48,48]{1,0:T(8,128)(2,1)} %head.1) | copy-start | bytes 13828
  15.7 6.0 %copy-start.2 = (f32[48]{0:T(128)S(1)}, f32[48]{0:T(128)}, u32[]{:S(2)}) copy-start(f32[48]{0:T(128)} %param.11) | copy-start | bytes 580
  15.7 6.0 %copy-start.3 = (f32[48]{0:T(128)S(1)}, f32[48]{0:T(128)}, u32[]{:S(2)}) copy-start(f32[48]{0:T(128)} %param.13) | copy-start | bytes 580
